TPU v7x, 128 devices: a whole 4x4x4 slice. The times are simulated.
128 devices in a mesh: dp: 16 (over z, y_hi, core), expert: 8 (over y_lo, x).
Axes of the slice: x: 4, y: 4 (y_hi: 2, y_lo: 2; y = y_hi * 2 + y_lo), z: 4, core: 2. Of those that a mesh axis runs over, the one named last changes fastest.
Arguments:
- tokens: bfloat16 [1536, 6144], P(('dp', 'expert')), may hold values from -6 to 6
- cotangent: bfloat16 [1536, 6144], P(('dp', 'expert')), may hold values from -6 to 6
- expert_ids: int32 [1536, 2], P('dp'), may hold values from 0 to 7, all different within a row; in each aligned block of 96 rows (0 to 95, 96 to 191, ...) at most 32 rows name the same one
- gate_values: float32 [1536, 2], P('dp'), may hold values from 0.2 to 1
- w_in: bfloat16 [8, 6144, 8192], P('expert', None, 'dp'), may hold values from -0.078125 to 0.078125
- w_out: bfloat16 [8, 8192, 6144], P('expert', 'dp'), may hold values from -0.0625 to 0.0625
Outputs:
- layer_out: bfloat16 [1536, 6144], P(('dp', 'expert'))
- grad_tokens: bfloat16 [1536, 6144], P(('dp', 'expert'))
- grad_in: bfloat16 [8, 6144, 8192], P('expert', None, 'dp')
- grad_out: bfloat16 [8, 8192, 6144], P('expert', 'dp')
Inputs may be any that keep to these rules, and one draw needn't show every extreme that they name: `expert_ids`: A token names 2 different experts. Within the 96 tokens of one dp index no expert is named by more than 32 tokens, and in every draw some expert is named by exactly 32 tokens of some dp index.
All inputs are finite; a program needn't handle non-finite values.
Results may differ from a plain program's by a relative error of at most 0.0058.
Values may be sent and summed in bfloat16 or wider, within the bound.
A program may use at most 192 MiB of HBM per device.

v0:
```python
import jax
import jax.numpy as jnp
from jax import lax
from jax.sharding import PartitionSpec as P


def slot_tables(ids, gates, expert, slot_count):
    chosen = ids == expert
    gate_sum = jnp.sum(jnp.where(chosen, gates, jnp.float32(0.0)), axis=1)
    picked = jnp.any(chosen, axis=1).astype(jnp.int32)
    placed = jnp.cumsum(picked) - 1
    slots = lax.broadcasted_iota(jnp.int32, (slot_count, ids.shape[0]), 0)
    table = ((placed[None, :] == slots) & (picked[None, :] == 1)).astype(jnp.float32)
    return (table, gate_sum)


def unpack(table, slot_rows):
    return jnp.dot(
        table.T, slot_rows, precision=lax.Precision.HIGHEST, preferred_element_type=jnp.float32
    )


def local(tokens, cotangent, expert_ids, gate_values, w_in, w_out):
    group_tokens = expert_ids.shape[0]
    slot_count = max(
        group_tokens // 3, expert_ids.shape[1] * group_tokens // lax.axis_size("expert")
    )
    expert = lax.axis_index("expert")
    table, gate_sum = slot_tables(expert_ids, gate_values, expert, slot_count)
    table_half = table.astype(jnp.bfloat16)
    weight_in = w_in[0]
    weight_out = w_out[0]
    group_in, group_cot = (
        lax.all_gather(tokens, "expert", axis=0, tiled=True),
        lax.all_gather(cotangent, "expert", axis=0, tiled=True),
    )
    packed = jnp.dot(table_half, group_in, preferred_element_type=jnp.float32).astype(jnp.bfloat16)
    rows = lax.all_gather(packed, "dp", axis=0, tiled=True)
    pre = jnp.dot(rows, weight_in, preferred_element_type=jnp.float32)
    hidden = jax.nn.silu(pre).astype(jnp.bfloat16)
    weighted = (gate_sum[:, None] * group_cot).astype(jnp.bfloat16)
    packed_grad = jnp.dot(table_half, weighted, preferred_element_type=jnp.float32).astype(
        jnp.bfloat16
    )
    piece = hidden
    slot_out = lax.psum_scatter(
        jnp.dot(piece, weight_out, preferred_element_type=jnp.float32),
        "dp",
        scatter_dimension=0,
        tiled=True,
    )
    out_term = gate_sum[:, None] * unpack(table, slot_out)
    layer_out = lax.psum_scatter(out_term, "expert", scatter_dimension=0, tiled=True).astype(
        jnp.bfloat16
    )
    row_keep, slot_grad = (
        lax.all_gather(packed, "dp", axis=0, tiled=True),
        lax.all_gather(packed_grad, "dp", axis=0, tiled=True),
    )
    grad_out = jnp.einsum("rf,rd->fd", hidden, slot_grad, preferred_element_type=jnp.float32)
    grad_hidden = jnp.einsum("rd,fd->rf", slot_grad, weight_out, preferred_element_type=jnp.float32)
    sig = jax.nn.sigmoid(pre)
    grad_pre = (grad_hidden * sig * (1.0 + pre * (1.0 - sig))).astype(jnp.bfloat16)
    grad_in = jnp.einsum("rd,rf->df", row_keep, grad_pre, preferred_element_type=jnp.float32)
    piece = grad_pre
    slot_back = lax.psum_scatter(
        jnp.einsum("rf,df->rd", piece, weight_in, preferred_element_type=jnp.float32),
        "dp",
        scatter_dimension=0,
        tiled=True,
    )
    back_term = unpack(table, slot_back)
    grad_tokens = lax.psum_scatter(back_term, "expert", scatter_dimension=0, tiled=True).astype(
        jnp.bfloat16
    )
    return (
        layer_out,
        grad_tokens,
        grad_in.astype(jnp.bfloat16)[None],
        grad_out.astype(jnp.bfloat16)[None],
    )


def solution(mesh):
    placed = (
        P(("dp", "expert"), None),
        P(("dp", "expert"), None),
        P("dp", None),
        P("dp", None),
        P("expert", None, "dp"),
        P("expert", "dp", None),
    )
    return jax.shard_map(
        local,
        mesh=mesh,
        in_specs=placed,
        out_specs=(
            P(("dp", "expert"), None),
            P(("dp", "expert"), None),
            P("expert", None, "dp"),
            P("expert", "dp", None),
        ),
        check_vma=False,
    )
```

profile of v0, /device:TPU:4, one launch (start us, length us, event | category | flops | bytes accessed | tf_op | source)
XLA Modules:
  0.0 590.6 jit_solution(5294595046763693529)
XLA Ops:
  9.8 40.8 %all-gather.11.cloned.1.call-done = bf16[8,12,6144]{2,1,0:T(8,128)(2,1)} async-done(((bf16[1,12,6144]{2,1,0:T(8,128)(2,1)}), bf16[8,12,6144]{2,1,0:T(8,128)(2,1)}) %all-gather.11.cloned.1.call-update) | async-done | bytes 1179664 | tf_op jit(solution)/shard_map/all_gather | solution.py:34
  50.5 1.5 reshape.48
  53.9 38.0 %all-gather.13.cloned.1.call-done = bf16[8,12,6144]{2,1,0:T(8,128)(2,1)} async-done(((bf16[1,12,6144]{2,1,0:T(8,128)(2,1)}), bf16[8,12,6144]{2,1,0:T(8,128)(2,1)}) %all-gather.13.cloned.1.call-update) | async-done | bytes 1179664 | tf_op jit(solution)/shard_map/all_gather | solution.py:35
  92.0 1.5 reshape.51
  93.5 1.1 convolution_convert_fusion.2
  94.7 65.8 %all-gather.7.cloned.1.call-done = bf16[512,6144]{1,0:T(8,128)(2,1)} async-done(((bf16[32,6144]{1,0:T(8,128)(2,1)}), bf16[512,6144]{1,0:T(8,128)(2,1)}) %all-gather.7.cloned.1.call-update) | async-done | bytes 6291472 | tf_op jit(solution)/shard_map/all_gather | solution.py:38
  160.5 7.5 %fusion.10 = f32[512,512]{1,0:T(8,128)S(1)} fusion(bf16[512,6144]{1,0:T(8,128)(2,1)} %all-gather.7.cloned.1.call-done, bf16[1,6144,512]{2,1,0:T(8,128)(2,1)} %param.10), kind=kOutput, calls=%fused_computation.13 | convolution fusion | flops 3221225472 | bytes 13631488 | tf_op jit(solution)/shard_map/dot_general | solution.py:39
  168.0 9.2 %fusion.6 = f32[512,6144]{1,0:T(8,128)} fusion(bf16[1,512,6144]{2,1,0:T(8,128)(2,1)} %param.11, f32[512,512]{1,0:T(8,128)S(1)} %fusion.10), kind=kOutput, calls=%fused_computation.9 | convolution fusion | flops 3222536192 | bytes 19922944 | tf_op jit(solution)/shard_map/dot_general | solution.py:47
  177.5 47.9 %all-gather.9.cloned.1.call-done = bf16[512,6144]{1,0:T(8,128)(2,1)} async-done(((bf16[32,6144]{1,0:T(8,128)(2,1)}), bf16[512,6144]{1,0:T(8,128)(2,1)}) %all-gather.9.cloned.1.call-update) | async-done | bytes 6291472 | tf_op jit(solution)/shard_map/all_gather | solution.py:58
  225.4 8.2 %fusion.18 = bf16[512,512]{1,0:T(8,128)(2,1)S(1)} fusion(bf16[512,6144]{1,0:T(8,128)(2,1)} %all-gather.9.cloned.1.call-done, bf16[1,512,6144]{2,1,0:T(8,128)(2,1)} %param.11, f32[512,512]{1,0:T(8,128)S(1)} %fusion.10), kind=kOutput, calls=%fused_computation.18 | convolution fusion | flops 3223584768 | bytes 14155776 | tf_op jit(solution)/shard_map/rd,fd->rf/dot_general | solution.py:61
  233.6 11.0 %fusion.8 = f32[512,6144]{1,0:T(8,128)} fusion(bf16[512,512]{1,0:T(8,128)(2,1)S(1)} %fusion.18, bf16[1,6144,512]{2,1,0:T(8,128)(2,1)} %param.10), kind=kOutput, calls=%fused_computation.11 | convolution fusion | flops 3221225472 | bytes 19398656 | tf_op jit(solution)/shard_map/rf,df->rd/dot_general | solution.py:67
  246.5 9.1 %fusion.2 = bf16[1,6144,512]{2,1,0:T(8,128)(2,1)} fusion(bf16[512,6144]{1,0:T(8,128)(2,1)} %all-gather.7.cloned.1.call-done, bf16[512,512]{1,0:T(8,128)(2,1)S(1)} %fusion.18), kind=kOutput, calls=%fused_computation.2 | convolution fusion | flops 3224371200 | bytes 13107200 | tf_op jit(solution)/shard_map/rd,rf->df/dot_general | solution.py:64
  255.6 94.1 %reduce-scatter.7.cloned.1.call-done = f32[32,6144]{1,0:T(8,128)} async-done(((f32[512,6144]{1,0:T(8,128)}), f32[32,6144]{1,0:T(8,128)}) %reduce-scatter.7.cloned.1.call-update) | async-done | bytes 786448 | tf_op jit(solution)/shard_map/reduce_scatter | solution.py:46
  349.7 2.3 convolution_multiply_fusion
  352.0 122.6 %reduce-scatter.9.cloned.1.call-done = f32[32,6144]{1,0:T(8,128)} async-done(((f32[512,6144]{1,0:T(8,128)}), f32[32,6144]{1,0:T(8,128)}) %reduce-scatter.9.cloned.1.call-update) | async-done | bytes 786448 | tf_op jit(solution)/shard_map/reduce_scatter | solution.py:66
  474.6 3.7 fusion.23
  478.3 72.7 %fusion.35 = (f32[16,6144]{1,0:T(8,128)}, f32[16,6144]{1,0:T(8,128)}) fusion(f32[96,6144]{1,0:T(8,128)S(1)} %convolution_multiply_fusion, f32[96,6144]{1,0:T(8,128)} %fusion.23), kind=kCustom, calls=%all-reduce-scatter.2 | all-reduce-scatter fusion | flops 1572865 | bytes 5505536
  553.0 2.6 collective-permute-start.2
  555.7 5.5 collective-permute-start.3
  561.2 8.2 %fusion.3 = bf16[1,512,6144]{2,1,0:T(8,128)(2,1)} fusion(bf16[512,6144]{1,0:T(8,128)(2,1)} %all-gather.9.cloned.1.call-done, f32[512,512]{1,0:T(8,128)S(1)} %fusion.10), kind=kOutput, calls=%fused_computation.3 | convolution fusion | flops 3225681920 | bytes 13631488 | tf_op jit(solution)/shard_map/rf,rd->fd/dot_general | solution.py:60
  569.5 2.5 collective-permute-start
  572.0 1.9 collective-permute-start.1
  574.0 1.1 concatenate.1
  575.8 6.2 %collective-permute-done.1 = bf16[12,6144]{1,0:T(8,128)(2,1)S(1)} collective-permute-done((bf16[12,6144]{1,0:T(8,128)(2,1)S(1)}, bf16[12,6144]{1,0:T(8,128)(2,1)S(1)}, u32[]{:S(2)}, u32[]{:S(2)}) %collective-permute-start.1) | collective-permute-done | bytes 147488
  (36 shorter events, 10.5 us)
Async XLA Ops:
  7.2 43.4 %all-gather.11.cloned.1.call-start = ((), (), s32[]{:S(2)}) async-start(), calls=%async_computation.6 | async-start | bytes 1769472 | tf_op jit(solution)/shard_map/all_gather | solution.py:34
  7.9 84.1 %all-gather.13.cloned.1.call-start = ((), (), s32[]{:S(2)}) async-start(), calls=%async_computation.7 | async-start | bytes 1769472 | tf_op jit(solution)/shard_map/all_gather | solution.py:35
  8.6 151.9 %all-gather.7.cloned.1.call-start = ((), (), s32[]{:S(2)}) async-start(), calls=%async_computation.2 | async-start | bytes 6684672 | tf_op jit(solution)/shard_map/all_gather | solution.py:38
  53.1 172.2 %all-gather.9.cloned.1.call-start = ((), (), s32[]{:S(2)}) async-start(), calls=%async_computation.4 | async-start | bytes 6684672 | tf_op jit(solution)/shard_map/all_gather | solution.py:58
  94.6 255.1 %reduce-scatter.7.cloned.1.call-start = ((), (), s32[]{:S(2)}) async-start(), calls=%async_computation.3 | async-start | bytes 13369344 | tf_op jit(solution)/shard_map/reduce_scatter | solution.py:46
  177.2 297.4 %reduce-scatter.9.cloned.1.call-start = ((), (), s32[]{:S(2)}) async-start(), calls=%async_computation.5 | async-start | bytes 13369344 | tf_op jit(solution)/shard_map/reduce_scatter | solution.py:66
  244.6 0.7 copy-start.2
  553.0 16.4 %copy-start = (f32[16,6144]{1,0:T(8,128)S(1)}, f32[16,6144]{1,0:T(8,128)}, u32[]{:S(2)}) copy-start(f32[16,6144]{1,0:T(8,128)} %get-tuple-element.6) | copy-start | bytes 1179652
  553.0 20.9 %copy-start.1 = (f32[16,6144]{1,0:T(8,128)S(1)}, f32[16,6144]{1,0:T(8,128)}, u32[]{:S(2)}) copy-start(f32[16,6144]{1,0:T(8,128)} %get-tuple-element.7) | copy-start | bytes 1179652
  553.0 20.9 %collective-permute-start.2 = (bf16[16,6144]{1,0:T(8,128)(2,1)S(1)}, bf16[16,6144]{1,0:T(8,128)(2,1)S(1)}, u32[]{:S(2)}, u32[]{:S(2)}) collective-permute-start(bf16[16,6144]{1,0:T(8,128)(2,1)S(1)} %convert.2), channel_id=1, source_target_pairs={{0,1},{1,2},{2,3},{3,4},{4,5},{5,6},{6,7},{8,9},{9,10},{10,11},{11... | collective-permute-start | bytes 589832
  555.7 18.2 %collective-permute-start.3 = (bf16[12,6144]{1,0:T(8,128)(2,1)S(1)}, bf16[12,6144]{1,0:T(8,128)(2,1)S(1)}, u32[]{:S(2)}, u32[]{:S(2)}) collective-permute-start(bf16[12,6144]{1,0:T(8,128)(2,1)S(1)} %slice.1), channel_id=1, source_target_pairs={{0,2},{1,3},{2,4},{3,5},{4,6},{5,7},{8,10},{9,11},{10,12},{11,13},... | collective-permute-start | bytes 442376
  569.5 12.5 %collective-permute-start = (bf16[16,6144]{1,0:T(8,128)(2,1)S(1)}, bf16[16,6144]{1,0:T(8,128)(2,1)S(1)}, u32[]{:S(2)}, u32[]{:S(2)}) collective-permute-start(bf16[16,6144]{1,0:T(8,128)(2,1)S(1)} %convert.1), channel_id=1, source_target_pairs={{0,1},{1,2},{2,3},{3,4},{4,5},{5,6},{6,7},{8,9},{9,10},{10,11},{11... | collective-permute-start | bytes 589832
  572.0 9.9 %collective-permute-start.1 = (bf16[12,6144]{1,0:T(8,128)(2,1)S(1)}, bf16[12,6144]{1,0:T(8,128)(2,1)S(1)}, u32[]{:S(2)}, u32[]{:S(2)}) collective-permute-start(bf16[12,6144]{1,0:T(8,128)(2,1)S(1)} %slice), channel_id=1, source_target_pairs={{0,2},{1,3},{2,4},{3,5},{4,6},{5,7},{8,10},{9,11},{10,12},{11,13},... | collective-permute-start | bytes 442376
Sparse Core Ops, SparseCore 0:
  9.6 40.8 all-gather.10
  52.2 39.7 all-gather.12
  95.0 65.4 all-gather.6
  163.4 61.9 all-gather.8
  229.5 120.1 reduce-scatter.6
  353.9 120.6 reduce-scatter.8
where the time goes:
time: 591 us
  waiting for transfers between devices  417 us (71%)
  blocking collectives  72.7 us (12%)
  matrix products  61.3 us (10%)
  between operations  14.9 us (3%)
  starting transfers between devices  13 us (2%)
  local copies, waits for them, and re-layouts  9.03 us (2%)
    reduce_scatter x1, waiting for transfers between devices, local(): lax.psum_scatter(jnp.einsum('rf,df->rd', piece, weight_in, preferred_elem...  123 us
    reduce_scatter x1, waiting for transfers between devices, local(): lax.psum_scatter(jnp.dot(piece, weight_out, preferred_element_type=jnp.fl...  94.1 us
    unnamed x1, blocking collectives  72.7 us
    all_gather x1, waiting for transfers between devices, local(): rows = lax.all_gather(packed, 'dp', axis=0, tiled=True)  65.8 us
    all_gather x1, waiting for transfers between devices, local(): lax.all_gather(packed_grad, 'dp', axis=0, tiled=True)  47.9 us
    all_gather x1, waiting for transfers between devices, local(): lax.all_gather(tokens, 'expert', axis=0, tiled=True)  40.8 us
    all_gather x1, waiting for transfers between devices, local(): lax.all_gather(cotangent, 'expert', axis=0, tiled=True)  38 us
    unnamed x4, starting transfers between devices  12.6 us
  transfers between devices with their start and end apart: 10, of which 7 were waited for; matrix products, arithmetic and copies ran while one was open for 11% of the time, Pallas kernels for 0%

commit v1 on v0

--- a/solution.py
+++ b/solution.py
@@ -35,7 +35,9 @@
         lax.all_gather(cotangent, "expert", axis=0, tiled=True),
     )
     packed = jnp.dot(table_half, group_in, preferred_element_type=jnp.float32).astype(jnp.bfloat16)
-    rows = lax.all_gather(packed, "dp", axis=0, tiled=True)
+    rows = jnp.concatenate(
+        lax.all_to_all(jnp.stack([packed] * lax.axis_size("dp")), "dp", 0, 0), axis=0
+    )
     pre = jnp.dot(rows, weight_in, preferred_element_type=jnp.float32)
     hidden = jax.nn.silu(pre).astype(jnp.bfloat16)
     weighted = (gate_sum[:, None] * group_cot).astype(jnp.bfloat16)

time: 591 us -> 633 us (1.071)
  blocking collectives: 72.7 us -> 175 us
  waiting for transfers between devices: 417 us -> 364 us
  matrix products: 61.3 us -> 52.1 us
    all_to_all x0 -> x1, blocking collectives: none -> 102 us  [local(): lax.all_to_all(jnp.stack([packed] * lax.axis_size('dp')), 'dp', 0, 0)]
    all_gather x1, waiting for transfers between devices: 47.9 us -> 0.02 us  [local(): lax.all_gather(packed_grad, 'dp', axis=0, tiled=True)]
    all_gather x1, waiting for transfers between devices: 65.8 us -> 38.4 us  [local(): lax.all_gather(packed, 'dp', axis=0, tiled=True)]
    reduce_scatter x1, waiting for transfers between devices: 94.1 us -> 116 us  [local(): lax.psum_scatter(jnp.dot(piece, weight_out, preferred_element_type=jnp.fl...]
  transfers between devices with their start and end apart: 10 -> 10, of which waited for: 7 -> 7; matrix products, arithmetic and copies ran while one was open for 11% -> 9% of each run, Pallas kernels for 0% -> 0%
where the time goes in v1:
time: 633 us
  waiting for transfers between devices  364 us (58%)
  blocking collectives  175 us (28%)
  matrix products  52.1 us (8%)
  between operations  15 us (2%)
  starting transfers between devices  13 us (2%)
  local copies, waits for them, and re-layouts  10.9 us (2%)
    reduce_scatter x1, waiting for transfers between devices, local(): lax.psum_scatter(jnp.einsum('rf,df->rd', piece, weight_in, preferred_elem...  123 us
    reduce_scatter x1, waiting for transfers between devices, local(): lax.psum_scatter(jnp.dot(piece, weight_out, preferred_element_type=jnp.fl...  116 us
    all_to_all x1, blocking collectives, local(): lax.all_to_all(jnp.stack([packed] * lax.axis_size('dp')), 'dp', 0, 0)  102 us
    unnamed x1, blocking collectives  72.7 us
    all_gather x1, waiting for transfers between devices, local(): lax.all_gather(cotangent, 'expert', axis=0, tiled=True)  40.1 us
    all_gather x1, waiting for transfers between devices, local(): lax.all_gather(tokens, 'expert', axis=0, tiled=True)  38.7 us
    all_gather x1, waiting for transfers between devices, local(): lax.all_gather(packed, 'dp', axis=0, tiled=True)  38.4 us
  transfers between devices with their start and end apart: 10, of which 7 were waited for; matrix products, arithmetic and copies ran while one was open for 9% of the time, Pallas kernels for 0%

profile of v1, /device:TPU:4, one launch (start us, length us, event | category | flops | bytes accessed | tf_op | source)
XLA Modules:
  0.0 632.6 jit_solution(17623139273616379257)
XLA Ops:
  10.5 40.1 %all-gather.13.cloned.1.call-done = bf16[8,12,6144]{2,1,0:T(8,128)(2,1)} async-done(((bf16[1,12,6144]{2,1,0:T(8,128)(2,1)}), bf16[8,12,6144]{2,1,0:T(8,128)(2,1)}) %all-gather.13.cloned.1.call-update) | async-done | bytes 1179664 | tf_op jit(solution)/shard_map/all_gather | solution.py:35
  50.5 1.5 reshape.57
  53.3 38.7 %all-gather.11.cloned.1.call-done = bf16[8,12,6144]{2,1,0:T(8,128)(2,1)} async-done(((bf16[1,12,6144]{2,1,0:T(8,128)(2,1)}), bf16[8,12,6144]{2,1,0:T(8,128)(2,1)}) %all-gather.11.cloned.1.call-update) | async-done | bytes 1179664 | tf_op jit(solution)/shard_map/all_gather | solution.py:34
  92.0 1.5 reshape.54
  94.6 1.9 stack.2
  96.6 102.3 %all_to_all.5 = bf16[16,32,6144]{2,1,0:T(8,128)(2,1)S(1)} all-to-all(bf16[16,32,6144]{2,1,0:T(8,128)(2,1)S(1)} %stack.2), channel_id=1, replica_groups=mesh['dp'=16,'expert'=8] {'dp'}, dimensions={0} | all-to-all | bytes 12582912 | tf_op jit(solution)/shard_map/all_to_all | solution.py:39
  198.8 3.4 fusion.10
  202.3 6.5 %fusion.6 = f32[512,6144]{1,0:T(8,128)} fusion(bf16[1,512,6144]{2,1,0:T(8,128)(2,1)S(1)} %bitcast.41, f32[512,512]{1,0:T(8,128)S(1)} %fusion.10), kind=kOutput, calls=%fused_computation.9 | convolution fusion | flops 3222536192 | bytes 19922944 | tf_op jit(solution)/shard_map/dot_general | solution.py:49
  209.0 8.5 %fusion.18 = bf16[512,512]{1,0:T(8,128)(2,1)S(1)} fusion(bf16[512,6144]{1,0:T(8,128)(2,1)} %all-gather.7.cloned.1.call-done, bf16[1,512,6144]{2,1,0:T(8,128)(2,1)} %param.11, f32[512,512]{1,0:T(8,128)S(1)} %fusion.10), kind=kOutput, calls=%fused_computation.18 | convolution fusion | flops 3223584768 | bytes 14155776 | tf_op jit(solution)/shard_map/rd,fd->rf/dot_general | solution.py:63
  217.5 9.2 %fusion.8 = f32[512,6144]{1,0:T(8,128)} fusion(bf16[512,512]{1,0:T(8,128)(2,1)S(1)} %fusion.18, bf16[1,6144,512]{2,1,0:T(8,128)(2,1)} %param.10), kind=kOutput, calls=%fused_computation.11 | convolution fusion | flops 3221225472 | bytes 19398656 | tf_op jit(solution)/shard_map/rf,df->rd/dot_general | solution.py:69
  228.6 38.4 %all-gather.9.cloned.1.call-done = bf16[512,6144]{1,0:T(8,128)(2,1)} async-done(((bf16[32,6144]{1,0:T(8,128)(2,1)}), bf16[512,6144]{1,0:T(8,128)(2,1)}) %all-gather.9.cloned.1.call-update) | async-done | bytes 6291472 | tf_op jit(solution)/shard_map/all_gather | solution.py:59
  267.0 8.2 %fusion.2 = bf16[1,6144,512]{2,1,0:T(8,128)(2,1)} fusion(bf16[512,6144]{1,0:T(8,128)(2,1)} %all-gather.9.cloned.1.call-done, bf16[512,512]{1,0:T(8,128)(2,1)S(1)} %fusion.18), kind=kOutput, calls=%fused_computation.2 | convolution fusion | flops 3224371200 | bytes 13107200 | tf_op jit(solution)/shard_map/rd,rf->df/dot_general | solution.py:66
  275.2 116.2 %reduce-scatter.7.cloned.1.call-done = f32[32,6144]{1,0:T(8,128)} async-done(((f32[512,6144]{1,0:T(8,128)}), f32[32,6144]{1,0:T(8,128)}) %reduce-scatter.7.cloned.1.call-update) | async-done | bytes 786448 | tf_op jit(solution)/shard_map/reduce_scatter | solution.py:48
  391.3 2.3 convolution_multiply_fusion
  393.6 122.6 %reduce-scatter.9.cloned.1.call-done = f32[32,6144]{1,0:T(8,128)} async-done(((f32[512,6144]{1,0:T(8,128)}), f32[32,6144]{1,0:T(8,128)}) %reduce-scatter.9.cloned.1.call-update) | async-done | bytes 786448 | tf_op jit(solution)/shard_map/reduce_scatter | solution.py:68
  516.2 3.7 fusion.23
  519.9 72.7 %fusion.35 = (f32[16,6144]{1,0:T(8,128)}, f32[16,6144]{1,0:T(8,128)}) fusion(f32[96,6144]{1,0:T(8,128)S(1)} %convolution_multiply_fusion, f32[96,6144]{1,0:T(8,128)} %fusion.23), kind=kCustom, calls=%all-reduce-scatter.2 | all-reduce-scatter fusion | flops 1572865 | bytes 5505536
  594.7 4.8 collective-permute-start.1
  599.5 3.9 collective-permute-start
  603.4 8.2 %fusion.3 = bf16[1,512,6144]{2,1,0:T(8,128)(2,1)} fusion(bf16[512,6144]{1,0:T(8,128)(2,1)} %all-gather.7.cloned.1.call-done, f32[512,512]{1,0:T(8,128)S(1)} %fusion.10), kind=kOutput, calls=%fused_computation.3 | convolution fusion | flops 3225681920 | bytes 13631488 | tf_op jit(solution)/shard_map/rf,rd->fd/dot_general | solution.py:62
  611.7 1.9 collective-permute-start.3
  613.6 1.9 collective-permute-start.2
  617.4 4.5 collective-permute-done.3
  621.9 2.0 collective-permute-done.2
  (48 shorter events, 12.8 us)
Async XLA Ops:
  7.2 43.4 %all-gather.13.cloned.1.call-start = ((), (), s32[]{:S(2)}) async-start(), calls=%async_computation.8 | async-start | bytes 1769472 | tf_op jit(solution)/shard_map/all_gather | solution.py:35
  7.9 84.1 %all-gather.11.cloned.1.call-start = ((), (), s32[]{:S(2)}) async-start(), calls=%async_computation.7 | async-start | bytes 1769472 | tf_op jit(solution)/shard_map/all_gather | solution.py:34
  8.6 200.4 %all-gather.7.cloned.1.call-start = ((), (), s32[]{:S(2)}) async-start(), calls=%async_computation.4 | async-start | bytes 6684672 | tf_op jit(solution)/shard_map/all_gather | solution.py:60
  53.2 213.8 %all-gather.9.cloned.1.call-start = ((), (), s32[]{:S(2)}) async-start(), calls=%async_computation.6 | async-start | bytes 6684672 | tf_op jit(solution)/shard_map/all_gather | solution.py:59
  94.6 296.8 %reduce-scatter.7.cloned.1.call-start = ((), (), s32[]{:S(2)}) async-start(), calls=%async_computation.3 | async-start | bytes 13369344 | tf_op jit(solution)/shard_map/reduce_scatter | solution.py:48
  94.6 104.2 %slice-start.2 = ((s8[6291456]{0:T(1024)(128)(4,1)}), s8[4194304]{0:T(1024)(128)(4,1)S(1)}, s32[]{:S(2)}) async-start(s8[6291456]{0:T(1024)(128)(4,1)} %bitcast.43), calls=%async_computation.11 | async-start | bytes 8388608
  96.5 102.3 %slice-start.3 = ((s8[6291456]{0:T(1024)(128)(4,1)}), s8[2097152]{0:T(1024)(128)(4,1)S(1)}, s32[]{:S(2)}) async-start(s8[6291456]{0:T(1024)(128)(4,1)} %bitcast.43), calls=%async_computation.12 | async-start | bytes 4194304
  96.5 105.7 %slice-start = ((s8[6291456]{0:T(1024)(128)(4,1)}), s8[4194304]{0:T(1024)(128)(4,1)S(1)}, s32[]{:S(2)}) async-start(s8[6291456]{0:T(1024)(128)(4,1)} %bitcast.40), calls=%async_computation.9 | async-start | bytes 8388608
  198.8 3.4 slice-start.1
  208.8 307.5 %reduce-scatter.9.cloned.1.call-start = ((), (), s32[]{:S(2)}) async-start(), calls=%async_computation.5 | async-start | bytes 13369344 | tf_op jit(solution)/shard_map/reduce_scatter | solution.py:68
  226.7 0.7 copy-start.2
  594.7 17.0 %copy-start = (f32[16,6144]{1,0:T(8,128)S(1)}, f32[16,6144]{1,0:T(8,128)}, u32[]{:S(2)}) copy-start(f32[16,6144]{1,0:T(8,128)} %get-tuple-element.7) | copy-start | bytes 1179652
  594.7 20.9 %copy-start.1 = (f32[16,6144]{1,0:T(8,128)S(1)}, f32[16,6144]{1,0:T(8,128)}, u32[]{:S(2)}) copy-start(f32[16,6144]{1,0:T(8,128)} %get-tuple-element.6) | copy-start | bytes 1179652
  594.7 20.9 %collective-permute-start.1 = (bf16[12,6144]{1,0:T(8,128)(2,1)S(1)}, bf16[12,6144]{1,0:T(8,128)(2,1)S(1)}, u32[]{:S(2)}, u32[]{:S(2)}) collective-permute-start(bf16[12,6144]{1,0:T(8,128)(2,1)S(1)} %slice), channel_id=1, source_target_pairs={{0,2},{1,3},{2,4},{3,5},{4,6},{5,7},{8,10},{9,11},{10,12},{11,13},... | collective-permute-start | bytes 442376
  599.5 16.1 %collective-permute-start = (bf16[16,6144]{1,0:T(8,128)(2,1)S(1)}, bf16[16,6144]{1,0:T(8,128)(2,1)S(1)}, u32[]{:S(2)}, u32[]{:S(2)}) collective-permute-start(bf16[16,6144]{1,0:T(8,128)(2,1)S(1)} %convert.1), channel_id=1, source_target_pairs={{0,1},{1,2},{2,3},{3,4},{4,5},{5,6},{6,7},{8,9},{9,10},{10,11},{11... | collective-permute-start | bytes 589832
  611.7 10.2 %collective-permute-start.3 = (bf16[12,6144]{1,0:T(8,128)(2,1)S(1)}, bf16[12,6144]{1,0:T(8,128)(2,1)S(1)}, u32[]{:S(2)}, u32[]{:S(2)}) collective-permute-start(bf16[12,6144]{1,0:T(8,128)(2,1)S(1)} %slice.1), channel_id=1, source_target_pairs={{0,2},{1,3},{2,4},{3,5},{4,6},{5,7},{8,10},{9,11},{10,12},{11,13},... | collective-permute-start | bytes 442376
  613.6 10.3 %collective-permute-start.2 = (bf16[16,6144]{1,0:T(8,128)(2,1)S(1)}, bf16[16,6144]{1,0:T(8,128)(2,1)S(1)}, u32[]{:S(2)}, u32[]{:S(2)}) collective-permute-start(bf16[16,6144]{1,0:T(8,128)(2,1)S(1)} %convert.2), channel_id=1, source_target_pairs={{0,1},{1,2},{2,3},{3,4},{4,5},{5,6},{6,7},{8,9},{9,10},{10,11},{11... | collective-permute-start | bytes 589832
Sparse Core Ops, SparseCore 0:
  9.6 40.8 all-gather.12
  52.2 39.7 all-gather.10
  95.0 107.6 all-gather.6
  205.6 61.3 all-gather.8
  271.2 120.1 reduce-scatter.6
  395.5 120.6 reduce-scatter.8
